TPU v7x, 256 devices: a whole 4x4x8 slice. The times are simulated.
256 devices in a mesh: dp: 64 (over x, y, z_hi), tensor: 4 (over z_lo, core).
Axes of the slice: x: 4, y: 4, z: 8 (z_hi: 4, z_lo: 2; z = z_hi * 2 + z_lo), core: 2. Of those that a mesh axis runs over, the one named last changes fastest.
Arguments:
- mlp_input: bfloat16 [64, 512, 4608], P('dp'), may hold values from -64 to 64
- mlp_cotangent: bfloat16 [64, 512, 36864], P('dp', None, 'tensor'), may hold values from -64 to 64
- head_outputs: bfloat16 [64, 512, 2048], P('dp', None, 'tensor'), may hold values from -64 to 64
- out_cotangent: bfloat16 [64, 512, 4608], P('dp'), may hold values from -64 to 64
Outputs:
- proj_gradient: float32 [4608, 2048], P('dp', 'tensor')
- clip_factors: float32 [64], P('dp')
All inputs are finite; a program needn't handle non-finite values.
Results may differ from a plain program's by a relative error of at most 0.0003.
Values may be sent and summed in bfloat16 or wider, within the bound.
A program may use at most 192 MiB of HBM per device.

v0:
```python
import math

import jax
import jax.numpy as jnp
from jax import lax
from jax.sharding import PartitionSpec as P

D = 4608
FF = 36864
HEAD_DIM = 128
HEADS = 16
SEQ = 512


def pair_gram(values):
    return jnp.einsum("btd,bsd->bts", values, values, preferred_element_type=jnp.float32)


def on_device(mlp_input, mlp_cotangent, head_outputs, out_cotangent):
    local_count = mlp_input.shape[0]
    examples = local_count * lax.axis_size("dp")
    threshold = 0.5 * SEQ * math.sqrt(D * FF + 4 * HEADS * HEAD_DIM * D)
    factor = math.sqrt(D * HEADS * HEAD_DIM / examples) / threshold
    mlp_part = jnp.sum(pair_gram(mlp_input) * pair_gram(mlp_cotangent), axis=(1, 2))
    example_grads = jnp.einsum(
        "btd,bth->bdh", out_cotangent, head_outputs, preferred_element_type=jnp.float32
    )
    attn_part = jnp.sum(example_grads * example_grads, axis=(1, 2))
    squared = lax.psum(mlp_part + attn_part, "tensor")
    clip_factors = threshold / jnp.maximum(jnp.sqrt(squared), threshold)
    weights = clip_factors * factor
    combined = jnp.einsum("bdh,b->dh", example_grads, weights)
    gradient = lax.psum_scatter(combined, "dp", scatter_dimension=0, tiled=True)
    return (gradient, clip_factors)


def solution(mesh):
    return jax.shard_map(
        on_device,
        mesh=mesh,
        in_specs=(
            P("dp", None, None),
            P("dp", None, "tensor"),
            P("dp", None, "tensor"),
            P("dp", None, None),
        ),
        out_specs=(P("dp", "tensor"), P("dp")),
        check_vma=False,
    )
```

profile of v0, /device:TPU:1, one launch (start us, length us, event | category | flops | bytes accessed | tf_op | source)
XLA Modules:
  0.0 318.6 jit_solution(13054636284949986217)
XLA Ops:
  7.2 0.0 copy-start
  7.2 0.0 reduce-scatter.2.cloned.1.call-start
  7.2 0.0 copy-start.1
  7.2 11.8 %fusion = f32[512,512]{1,0:T(8,128)S(1)} fusion(bf16[1,512,9216]{2,1,0:T(8,128)(2,1)} %param.5), kind=kOutput, calls=%fused_computation | convolution fusion | flops 4831838208 | bytes 10485760 | tf_op jit(solution)/shard_map/btd,bsd->bts/dot_general | solution.py:16
  19.1 0.0 copy-done.1
  19.1 0.0 copy-start.2
  19.1 3.4 %fusion.9 = f32[]{:T(128)} fusion(f32[512,512]{1,0:T(8,128)S(1)} %fusion, bf16[1,512,4608]{2,1,0:T(8,128)(2,1)S(1)} %copy-done.1), kind=kOutput, calls=%fused_computation.9 | convolution fusion | flops 2416443392 | bytes 5767172 | tf_op jit(solution)/shard_map/btd,bsd->bts/dot_general | solution.py:16
  22.5 0.0 copy-done
  22.5 0.0 copy-done.2
  22.5 6.3 %multiply_reduce_fusion = (f32[]{:T(128)}, f32[4608,512]{1,0:T(8,128)}) fusion(bf16[1,512,512]{2,1,0:T(8,128)(2,1)S(1)} %copy-done, bf16[1,512,4608]{2,1,0:T(8,128)(2,1)S(1)} %copy-done.2), kind=kOutput, calls=%fused_computation.2 | convolution fusion | flops 2420637696 | bytes 14680068 | tf_op jit(solution)/shard_map/btd,bth->bdh/dot_general | solution.py:25
  30.1 9.4 %psum.7 = f32[1]{0:T(128)} all-reduce(f32[1]{0:T(128)} %bitcast.4), channel_id=1, replica_groups=mesh['dp'=64,'tensor'=4] {'tensor'}, use_global_device_ids=true, to_apply=%region_2.0 | all-reduce | flops 1 | bytes 8 | tf_op jit(solution)/shard_map/psum | solution.py:29
  40.2 8.5 %broadcast_multiply_fusion = f32[4608,512]{1,0:T(8,128)} fusion(f32[4608,512]{1,0:T(8,128)} %get-tuple-element.3, f32[]{:T(128)} %bitcast.5), kind=kLoop, calls=%fused_computation.7 | loop fusion | flops 2359296 | bytes 18874372 | tf_op jit(solution)/shard_map/bdh,b->dh/dot_general | solution.py:32
  48.7 0.0 reduce-scatter.2.cloned.1.call-update
  48.7 261.9 %reduce-scatter.2.cloned.1.call-done = f32[72,512]{1,0:T(8,128)} async-done(((f32[4608,512]{1,0:T(8,128)}), f32[72,512]{1,0:T(8,128)}) %reduce-scatter.2.cloned.1.call-update) | async-done | bytes 147472 | tf_op jit(solution)/shard_map/reduce_scatter | solution.py:33
Async XLA Ops:
  7.2 15.3 %copy-start = (bf16[1,512,512]{2,1,0:T(8,128)(2,1)S(1)}, bf16[1,512,512]{2,1,0:T(8,128)(2,1)}, u32[]{:S(2)}) copy-start(bf16[1,512,512]{2,1,0:T(8,128)(2,1)} %param.6) | copy-start | bytes 1572868
  7.2 303.4 %reduce-scatter.2.cloned.1.call-start = ((), (), s32[]{:S(2)}) async-start(), calls=%async_computation.1 | async-start | bytes 9584640 | tf_op jit(solution)/shard_map/reduce_scatter | solution.py:33
  7.2 11.9 %copy-start.1 = (bf16[1,512,4608]{2,1,0:T(8,128)(2,1)S(1)}, bf16[1,512,4608]{2,1,0:T(8,128)(2,1)}, u32[]{:S(2)}) copy-start(bf16[1,512,4608]{2,1,0:T(8,128)(2,1)} %param.4) | copy-start | bytes 14155780
  19.1 3.4 %copy-start.2 = (bf16[1,512,4608]{2,1,0:T(8,128)(2,1)S(1)}, bf16[1,512,4608]{2,1,0:T(8,128)(2,1)}, u32[]{:S(2)}) copy-start(bf16[1,512,4608]{2,1,0:T(8,128)(2,1)} %param.7) | copy-start | bytes 14155780
Sparse Core Ops, SparseCore 0:
  48.8 261.7 reduce-scatter.1
where the time goes:
time: 320 us; the launch traced here: 319 us
  waiting for transfers between devices  262 us (82%)
  matrix products  21.5 us (7%)
  between operations  17.2 us (5%)
  blocking collectives  9.36 us (3%)
  other arithmetic  8.5 us (3%)
    reduce_scatter x1, waiting for transfers between devices, on_device(): gradient = lax.psum_scatter(combined, 'dp', scatter_dimension=0, tiled=True)  262 us
    dot_general x2, matrix products, pair_gram(): jnp.einsum('btd,bsd->bts', values, values, preferred_element_type=jnp.flo...  15.2 us
    psum x1, blocking collectives, on_device(): squared = lax.psum(mlp_part + attn_part, 'tensor')  9.36 us
    dot_general x1, other arithmetic, on_device(): combined = jnp.einsum('bdh,b->dh', example_grads, weights)  8.5 us
  transfers between devices with their start and end apart: 1, of which 1 were waited for; matrix products, arithmetic and copies ran while one was open for 0% of the time, Pallas kernels for 0%

commit v1 on v0

v1 whole, which is shorter than its diff:
```python
import functools
import itertools
import math

import jax
import jax.numpy as jnp
from jax import lax
from jax.experimental import pallas as pl
from jax.experimental.pallas import tpu as pltpu
from jax.sharding import PartitionSpec as P

D = 4608
FF = 36864
HD = 2048
SEQ = 512
EXAMPLES = 64
OWNED = D // EXAMPLES
COLS = 512
LANES = 128
HALF = SEQ // 2
MESH = pl.DeviceIdType.MESH

X0, X1, Y0, Y1, Z0, Z1 = (0, 0), (0, 1), (1, 0), (1, 1), (2, 0), (2, 1)
TURNS = (X0, X1, Y0, Y1, Z0, Z1)
ALONG_Z = (Z0, Z1)
PLANE = (X0, X1, Y0, Y1)
ORDERS = (
    ((X0,), (Y0,), (X1, Y1), ALONG_Z),
    ((Y0,), (X1,), (Y1, X0), ALONG_Z),
    ((X1,), (Y1,), (X0, Y0), ALONG_Z),
    ((Y1,), (X0,), (Y0, X1), ALONG_Z),
    ((Z0,), (Z1,), PLANE),
    ((Z1,), (Z0,), PLANE),
)
PARTS = (
    (0, 0, 32, 0),
    (1, 32, 24, 0),
    (2, 0, 32, 1),
    (3, 32, 24, 1),
    (4, 56, 16, 0),
    (5, 56, 16, 1),
    (1, 0, 32, 2),
    (0, 32, 24, 2),
    (3, 0, 32, 3),
    (2, 32, 24, 3),
    (4, 56, 16, 2),
    (5, 56, 16, 3),
)
XY = ((0, 1, 2, 3), (6, 7, 8, 9))
Z = ((4, 5), (10, 11))
Z_ALL = Z[0] + Z[1]
SCALE_ROWS = 16
POWER = 12
TOP = 1400.0
UP = 1.004
TINY = 1e-30


def layout():
    table, row = {}, 0

    def add(key, rows, turns):
        nonlocal row
        table[key] = (row, rows, turns)
        row += rows + SCALE_ROWS

    def reached(turns):
        for tau in range(1, 1 << len(turns)):
            bits = [(tau >> (len(turns) - 1 - i)) & 1 for i in range(len(turns))]
            yield tau, tuple(t for t, b in zip(turns, bits) if b)

    for p, (order, _, rows, _) in enumerate(PARTS):
        steps = ORDERS[order]
        add((p, 0, 1), 32 * rows, steps[0])
        add((p, 1, 1), 16 * rows, steps[1])
        if len(steps) == 4:
            for tau, turns in reached(steps[2]):
                add((p, 2, tau), 4 * rows, turns)
    for half in range(2):
        for tau, turns in reached(ALONG_Z):
            add(("xy", half, tau), sum(PARTS[p][2] for p in XY[half]), turns)
    for tau, turns in reached(PLANE):
        add(("z", 0, tau), sum(PARTS[p][2] for p in Z_ALL), turns)
    return table, row


MESSAGES, MESSAGE_ROWS = layout()
NUMBER = {key: i for i, key in enumerate(MESSAGES)}


def turn(v, kind, bit):
    step = 1 - 2 * lax.rem(v, 2) if kind == 0 else 3 - 2 * v
    return v + bit * step


def tiles(block):
    return block.reshape(block.shape[0] // 8, 8, block.shape[1])


def flat(block):
    return block.reshape(block.shape[0] * 8, block.shape[2])


def encode(block, inverse):
    v = tiles(block) * inverse[None]
    v2 = v * v
    v4 = v2 * v2
    power = v4 * v4 * v4
    return flat(jnp.where(v < 0, -power, power)).astype(jnp.bfloat16)


def decode(power, scale):
    v = jnp.exp2(jnp.log2(jnp.abs(power)) * (1.0 / POWER))
    return flat(tiles(jnp.where(power < 0, -v, v)) * scale[None])


def kernel(
    threshold,
    factor,
    mlp_in,
    mlp_cot,
    heads_in,
    out_cot,
    grad,
    clip,
    x_buf,
    c_buf,
    h_buf,
    o_buf,
    prod,
    gram_x,
    gram_c,
    squares,
    largest,
    bounds,
    outgoing,
    incoming,
    norm_out,
    norm_mate,
    norms,
    weights,
    in_sem,
    o_sem,
    c_sem,
    send_sem,
    recv_sem,
    mate_send,
    mate_recv,
    norm_send,
    norm_recv,
):
    me_dp = lax.axis_index("dp")
    me_t = lax.axis_index("tensor")
    core = lax.rem(me_t, 2)
    chip = lax.div(me_t, 2)
    place = (lax.div(me_dp, 16), lax.rem(lax.div(me_dp, 4), 4), lax.rem(me_dp, 4))

    def index_of(at):
        return at[0] * 16 + at[1] * 4 + at[2]

    def turned(turns):
        at = list(place)
        for axis, kind in turns:
            at[axis] = turn(at[axis], kind, 1)
        return index_of(at)

    o_step, c_step = 1536, D
    blocks = D // o_step

    def columns(source, target, start, size, sem):
        return pltpu.make_async_copy(
            source.at[0, :, pl.ds(start, size)], target.at[:, pl.ds(start, size)], sem
        )

    h_copy = pltpu.make_async_copy(heads_in.at[0], h_buf, in_sem.at[0])
    x_copy = pltpu.make_async_copy(mlp_in.at[0], x_buf, in_sem.at[1])
    o_copies = [columns(out_cot, o_buf, i * o_step, o_step, o_sem.at[i]) for i in range(blocks)]
    c_copies = [columns(mlp_cot, c_buf, i * c_step, c_step, c_sem.at[i]) for i in range(2)]
    for copy in [h_copy, *o_copies, x_copy, *c_copies]:
        copy.start()

    barrier = pltpu.get_barrier_semaphore()
    other_chip = lax.rem(me_t + 2, 4)
    other_core = (me_dp, turn(me_t, 0, 1))
    subsets = [s for n in range(1, 5) for s in itertools.combinations(PLANE, n)]
    subsets += [(Z0,), (Z1,), ALONG_Z]
    greeted = [(turned(s), me_t) for s in subsets]
    greeted += [(turned((t,)), other_chip) for t in TURNS]
    greeted += [(me_dp, other_chip), other_core]
    for device in greeted:
        pl.semaphore_signal(barrier, inc=1, device_id=device, device_id_type=MESH)

    def rows_of_message(key, ref):
        start, rows, _ = MESSAGES[key]
        return ref.at[pl.ds(start, rows + SCALE_ROWS)]

    def message(key):
        n = NUMBER[key]
        return pltpu.make_async_remote_copy(
            src_ref=rows_of_message(key, outgoing),
            dst_ref=rows_of_message(key, incoming),
            send_sem=send_sem.at[n],
            recv_sem=recv_sem.at[n],
            device_id=(turned(MESSAGES[key][2]), me_t),
            device_id_type=MESH,
        )

    def put_scale(key, sent):
        start, rows, _ = MESSAGES[key]
        outgoing[pl.ds(start + rows, SCALE_ROWS), :] = jnp.concatenate([sent, sent], axis=0)

    def put(key, at, block, inverse):
        start = MESSAGES[key][0]
        outgoing[pl.ds(pl.multiple_of(start + at, 16), block.shape[0]), :] = encode(block, inverse)

    def scale_in(key):
        start, rows, _ = MESSAGES[key]
        return incoming[pl.ds(start + rows, SCALE_ROWS), :].astype(jnp.float32)[:8]

    def got(key, at, size, scale):
        start = pl.multiple_of(MESSAGES[key][0] + at, 16)
        return decode(incoming[pl.ds(start, size), :].astype(jnp.float32), scale)

    def got_within(key, at, size, scale):
        low, high = at // 16 * 16, -(-(at + size) // 16) * 16
        raw = incoming[pl.ds(MESSAGES[key][0] + low, high - low), :].astype(jnp.float32)
        return decode(raw[at - low : at - low + size], scale)

    def to_send(bound):
        sent = (bound * UP).astype(jnp.bfloat16)
        return sent, 1.0 / sent.astype(jnp.float32)

    def lanes_of(p):
        return pl.ds(PARTS[p][3] * LANES, LANES)

    def place_of(p, done, group, k):
        order = list(itertools.chain(*ORDERS[PARTS[p][0]][done:]))
        at = list(place)
        for i, (axis, kind) in enumerate(order):
            weight = 1 << (len(order) - 1 - i)
            if weight >= 4:
                at[axis] = turn(at[axis], kind, lax.rem(lax.div(group, weight // 4), 2))
            elif (k // weight) % 2:
                at[axis] = turn(at[axis], kind, 1)
        start = index_of(at) * OWNED + PARTS[p][1]
        return pl.ds(pl.multiple_of(start, 8), PARTS[p][2])

    def own(p, done, group, ks):
        return jnp.concatenate([prod[place_of(p, done, group, k), lanes_of(p)] for k in ks], axis=0)

    def keep(p, done, group, ks, block):
        rows = PARTS[p][2]
        for i, k in enumerate(ks):
            prod[place_of(p, done, group, k), lanes_of(p)] = block[i * rows : (i + 1) * rows]

    ALL4 = range(4)
    h_copy.wait()
    for half in range(2):
        part = pl.ds(half * 256, 256)
        for i in range(blocks):
            if half == 0:
                o_copies[i].wait()
            block = lax.dot_general(
                o_buf[:, pl.ds(i * o_step, o_step)],
                h_buf[:, part],
                (((0,), (0,)), ((), ())),
                preferred_element_type=jnp.float32,
            )
            prod[pl.ds(i * o_step, o_step), part] = block
            block = tiles(block)
            square = jnp.sum(block * block, axis=0)
            most = jnp.max(jnp.abs(block), axis=0)
            squares[:, part] = square if i == 0 else squares[:, part] + square
            largest[:, part] = most if i == 0 else jnp.maximum(largest[:, part], most)
        if half == 0:
            pl.semaphore_wait(barrier, len(greeted))
        for p in Z[half] + XY[half]:
            rows = PARTS[p][2]
            bound = jnp.maximum(largest[:, lanes_of(p)] * (1.0 / TOP), TINY)
            bounds[p] = bound
            sent, inverse = to_send(bound)
            put_scale((p, 0, 1), sent)

            def first(g, carry, p=p, rows=rows, inverse=inverse):
                put((p, 0, 1), g * 4 * rows, own(p, 0, g + 8, ALL4), inverse)
                return carry

            lax.fori_loop(0, 8, first, 0)
            message((p, 0, 1)).start()

    nt = (((1,), (1,)), ((), ()))

    def gram(a, b):
        return lax.dot_general(a, b, nt, preferred_element_type=jnp.float32)

    x_copy.wait()
    mine = x_buf[pl.ds(pl.multiple_of(core * HALF, HALF), HALF), :]
    gram_x[core] = gram(mine, mine)
    quarter = pl.ds(pl.multiple_of(core * 128, 128), 128)
    gram_x[2, quarter, :] = gram(x_buf[quarter, :], x_buf[pl.ds(HALF, HALF), :])

    def to_core(source, target, n):
        return pltpu.make_async_remote_copy(
            src_ref=source,
            dst_ref=target,
            send_sem=mate_send.at[n],
            recv_sem=mate_recv.at[n],
            device_id=other_core,
            device_id_type=MESH,
        )

    grams_out = [
        to_core(gram_x.at[core], gram_x.at[core], 0),
        to_core(gram_x.at[2, quarter], gram_x.at[2, quarter], 1),
    ]
    for copy in grams_out:
        copy.start()
    attn = squares[...]
    partial = (attn[:, :128] + attn[:, 128:256]) + (attn[:, 256:384] + attn[:, 384:])
    for i in range(2):
        c_copies[i].wait()
        low = c_buf[pl.ds(0, HALF), pl.ds(i * c_step, c_step)]
        high = c_buf[pl.ds(HALF, HALF), pl.ds(i * c_step, c_step)]
        for j, (a, b) in enumerate(((low, low), (high, high), (low, high))):
            block = gram(a, b)
            gram_c[j] = block if i == 0 else gram_c[j] + block
    for copy in grams_out:
        copy.wait()
    both = gram_x[0] * gram_c[0] + gram_x[1] * gram_c[1] + 2.0 * (gram_x[2] * gram_c[2])
    both = jnp.sum(tiles(both), axis=0)
    norm_out[0] = partial + (both[:, :128] + both[:, 128:])
    mate = to_core(norm_out.at[0], norm_mate, 2)
    mate.start()
    mate.wait_recv()
    norm_out[1] = norm_out[0] + norm_mate[...]
    norms[0, chip] = norm_out[1]
    norm_copies = []
    for device, slot in [((me_dp, other_chip), 0)] + [
        ((turned((t,)), to), i + 1) for i, t in enumerate(TURNS) for to in (me_t, other_chip)
    ]:
        n = len(norm_copies)
        norm_copies.append(
            pltpu.make_async_remote_copy(
                src_ref=norm_out.at[1],
                dst_ref=norms.at[slot, chip],
                send_sem=norm_send.at[n],
                recv_sem=norm_recv.at[n],
                device_id=device,
                device_id_type=MESH,
            )
        )
    for copy in norm_copies:
        copy.start()
    for copy in norm_copies:
        copy.wait_recv()
    total = norms[:, 0] + norms[:, 1]
    total = jnp.sum(jnp.sum(total, axis=2, keepdims=True), axis=1, keepdims=True)
    factors = threshold / jnp.maximum(jnp.sqrt(jnp.broadcast_to(total, (7, 8, 128))), threshold)
    weights[...] = factors * factor

    def second(parts):
        kept = []
        for p in parts:
            order, _, rows, _ = PARTS[p]
            came = (p, 0, 1)
            message(came).wait_recv()
            mine = weights[0]
            scale = scale_in(came) * weights[1 + TURNS.index(ORDERS[order][0][0])]
            bound = bounds[p] * mine + scale
            bounds[p] = bound
            sent, inverse = to_send(bound)
            put_scale((p, 1, 1), sent)

            def summed(g, p=p, rows=rows, came=came, mine=mine, scale=scale):
                block = flat(tiles(own(p, 1, g, ALL4)) * mine[None])
                return block + got(came, g * 4 * rows, 4 * rows, scale)

            def send(g, carry, p=p, rows=rows, inverse=inverse, summed=summed):
                put((p, 1, 1), g * 4 * rows, summed(g + 4), inverse)
                return carry

            lax.fori_loop(0, 4, send, 0)
            message((p, 1, 1)).start()
            kept.append((p, summed))
        for p, summed in kept:

            def hold(g, carry, p=p, summed=summed):
                keep(p, 1, g, ALL4, summed(g))
                return carry

            lax.fori_loop(0, 4, hold, 0)

    def third(parts):
        kept = []
        for p in parts:
            rows = PARTS[p][2]
            came = (p, 1, 1)
            message(came).wait_recv()
            scale = scale_in(came)
            bound = bounds[p] + scale
            bounds[p] = bound
            sent, inverse = to_send(bound)

            def summed(g, p=p, rows=rows, came=came, scale=scale):
                return own(p, 2, g, ALL4) + got(came, g * 4 * rows, 4 * rows, scale)

            for tau in range(1, 4):
                put_scale((p, 2, tau), sent)
                put((p, 2, tau), 0, summed(tau), inverse)
                message((p, 2, tau)).start()
            kept.append((p, summed))
        for p, summed in kept:
            keep(p, 2, 0, ALL4, summed(0))

    def fourth(half):
        scales, bound = {}, None
        for p in XY[half]:
            here = bounds[p]
            for tau in range(1, 4):
                message((p, 2, tau)).wait_recv()
                scales[p, tau] = scale_in((p, 2, tau))
                here = here + scales[p, tau]
            bound = here if bound is None else jnp.maximum(bound, here)
        sent, inverse = to_send(bound)

        def summed(p, k):
            rows = PARTS[p][2]
            block = own(p, 3, 0, (k,))
            for tau in range(1, 4):
                block = block + got_within((p, 2, tau), k * rows, rows, scales[p, tau])
            return block

        for k in range(1, 4):
            key = ("xy", half, k)
            put_scale(key, sent)
            put(key, 0, jnp.concatenate([summed(p, k) for p in XY[half]], axis=0), inverse)
            message(key).start()
        for p in XY[half]:
            keep(p, 3, 0, (0,), summed(p, 0))

    def third_z():
        scales, bound = {}, None
        for p in Z_ALL:
            message((p, 1, 1)).wait_recv()
            scales[p] = scale_in((p, 1, 1))
            here = bounds[p] + scales[p]
            bound = here if bound is None else jnp.maximum(bound, here)
        sent, inverse = to_send(bound)

        def summed(p, g, ks):
            rows = PARTS[p][2]
            return own(p, 2, g, ks) + got((p, 1, 1), g * 4 * rows + ks[0] * rows, len(ks) * rows, scales[p])

        for owner in range(1, 16):
            key = ("z", 0, owner)
            put_scale(key, sent)
            put(
                key,
                0,
                jnp.concatenate([summed(p, owner // 4, (owner % 4,)) for p in Z_ALL], axis=0),
                inverse,
            )
            message(key).start()
        for p in Z_ALL:
            keep(p, 2, 0, (0,), summed(p, 0, (0,)))

    def finish(parts, kind, half, count):
        done = len(ORDERS[PARTS[parts[0]][0]])
        block = jnp.concatenate([own(p, done, 0, (0,)) for p in parts], axis=0)
        for tau in range(1, count):
            key = (kind, half, tau)
            message(key).wait_recv()
            block = block + got(key, 0, block.shape[0], scale_in(key))
        row = 0
        for p in parts:
            _, first_row, rows, _ = PARTS[p]
            grad[pl.ds(first_row, rows), lanes_of(p)] = block[row : row + rows]
            row += rows

    second(XY[0])
    second(XY[1])
    second(Z_ALL)
    third(XY[0])
    third(XY[1])
    fourth(0)
    third_z()
    fourth(1)
    finish(XY[0], "xy", 0, 4)
    finish(Z_ALL, "z", 0, 16)
    finish(XY[1], "xy", 1, 4)
    clip[0] = factors[0, 0, 0]
    for key in MESSAGES:
        message(key).wait_send()
    for copy in [mate, *norm_copies]:
        copy.wait_send()


def on_device(mlp_input, mlp_cotangent, head_outputs, out_cotangent):
    threshold = 0.5 * SEQ * math.sqrt(D * FF + 4 * HD * D)
    factor = math.sqrt(D * HD / EXAMPLES) / threshold
    f32, bf16 = jnp.float32, jnp.bfloat16
    dma = pltpu.SemaphoreType.DMA
    return pl.pallas_call(
        functools.partial(kernel, threshold, factor),
        out_shape=(
            jax.ShapeDtypeStruct((OWNED, COLS), f32),
            jax.ShapeDtypeStruct((1,), f32),
        ),
        in_specs=[pl.BlockSpec(memory_space=pl.ANY)] * 4,
        out_specs=(
            pl.BlockSpec(memory_space=pltpu.VMEM),
            pl.BlockSpec(memory_space=pltpu.SMEM),
        ),
        scratch_shapes=[
            pltpu.VMEM((SEQ, D), bf16),
            pltpu.VMEM((SEQ, FF // 4), bf16),
            pltpu.VMEM((SEQ, COLS), bf16),
            pltpu.VMEM((SEQ, D), bf16),
            pltpu.VMEM((D, COLS), f32),
            pltpu.VMEM((3, HALF, HALF), f32),
            pltpu.VMEM((3, HALF, HALF), f32),
            pltpu.VMEM((8, COLS), f32),
            pltpu.VMEM((8, COLS), f32),
            pltpu.VMEM((len(PARTS), 8, LANES), f32),
            pltpu.VMEM((MESSAGE_ROWS, LANES), bf16),
            pltpu.VMEM((MESSAGE_ROWS, LANES), bf16),
            pltpu.VMEM((2, 8, LANES), f32),
            pltpu.VMEM((8, LANES), f32),
            pltpu.VMEM((7, 2, 8, LANES), f32),
            pltpu.VMEM((7, 8, LANES), f32),
            dma((2,)),
            dma((3,)),
            dma((2,)),
            dma((len(MESSAGES),)),
            dma((len(MESSAGES),)),
            dma((3,)),
            dma((3,)),
            dma((13,)),
            dma((13,)),
        ],
        compiler_params=pltpu.CompilerParams(
            collective_id=0,
            has_side_effects=True,
            vmem_limit_bytes=56 * 2**20,
        ),
    )(mlp_input, mlp_cotangent, head_outputs, out_cotangent)


def solution(mesh):
    return jax.shard_map(
        on_device,
        mesh=mesh,
        in_specs=(
            P("dp", None, None),
            P("dp", None, "tensor"),
            P("dp", None, "tensor"),
            P("dp", None, None),
        ),
        out_specs=(P("dp", "tensor"), P("dp")),
        check_vma=False,
    )
```

time: 320 us -> 56 us (0.17)
  waiting for transfers between devices: 262 us -> 0 us
  Pallas kernels: 0 us -> 51.9 us
  matrix products: 21.5 us -> 0 us
  between operations: 17.2 us -> 2.39 us
  blocking collectives: 9.36 us -> 0 us
  other arithmetic: 8.5 us -> 0 us
    reduce_scatter x1 -> x0, waiting for transfers between devices: 262 us -> none  [on_device(): gradient = lax.psum_scatter(combined, 'dp', scatter_dimension=0, tiled=True)]
    pallas_call x0 -> x1, Pallas kernels: none -> 51.9 us  [on_device(): pl.pallas_call(functools.partial(kernel, threshold, factor), out_shape=(j...]
    dot_general x3 -> x0, matrix products: 21.5 us -> none  [the longest x2 15.2 us: pair_gram(): jnp.einsum('btd,bsd->bts', values, values, preferred_element_type=jnp.flo...]
    psum x1 -> x0, blocking collectives: 9.36 us -> none  [on_device(): squared = lax.psum(mlp_part + attn_part, 'tensor')]
    dot_general x1 -> x0, other arithmetic: 8.5 us -> none  [on_device(): combined = jnp.einsum('bdh,b->dh', example_grads, weights)]
  transfers between devices with their start and end apart: 1 -> 0, of which waited for: 1 -> 0; matrix products, arithmetic and copies ran while one was open for 0% -> 0% of each run, Pallas kernels for 0% -> 0%
where the time goes in v1:
time: 56 us; the launch traced here: 55.9 us
  Pallas kernels  51.9 us (93%)
  between operations  2.39 us (4%)
  local copies, waits for them, and re-layouts  1.58 us (3%)
    pallas_call x1, Pallas kernels, on_device(): pl.pallas_call(functools.partial(kernel, threshold, factor), out_shape=(j...  51.9 us
    unnamed x1, local copies, waits for them, and re-layouts  1.58 us

profile of v1, /device:TPU:1, one launch (start us, length us, event | category | flops | bytes accessed | tf_op | source)
XLA Modules:
  0.0 55.9 jit_solution(13313763460197272327)
XLA Ops:
  0.6 51.9 %shard_map.59 = (f32[72,512]{1,0:T(8,128)}, f32[1]{0:T(128)}) custom-call(bf16[1,512,4608]{2,1,0:T(8,128)(2,1)} %mlp_in.1, bf16[1,512,9216]{2,1,0:T(8,128)(2,1)} %mlp_cot.1, bf16[1,512,512]{2,1,0:T(8,128)(2,1)} %heads_in.1, bf16[1,512,4608]{2,1,0:T(8,128)(2,1)} %out_cot.1), custom_call_target="tpu_custom_call" | custom-call | tf_op jit(solution)/shard_map/pallas_call | solution.py:503
  52.6 1.6 %copy.8 = f32[72,512]{1,0:T(8,128)} copy(f32[72,512]{1,0:T(8,128)} %get-tuple-element.4) | data formatting | bytes 294912

commit v2 on v1

--- a/solution.py
+++ b/solution.py
@@ -210,16 +210,14 @@
         outgoing[pl.ds(start + rows, SCALE_ROWS), :] = jnp.concatenate([sent, sent], axis=0)
 
     def put(key, at, block, inverse):
-        start = MESSAGES[key][0]
-        outgoing[pl.ds(pl.multiple_of(start + at, 16), block.shape[0]), :] = encode(block, inverse)
+        outgoing[pl.ds(MESSAGES[key][0] + at, block.shape[0]), :] = encode(block, inverse)
 
     def scale_in(key):
         start, rows, _ = MESSAGES[key]
         return incoming[pl.ds(start + rows, SCALE_ROWS), :].astype(jnp.float32)[:8]
 
     def got(key, at, size, scale):
-        start = pl.multiple_of(MESSAGES[key][0] + at, 16)
-        return decode(incoming[pl.ds(start, size), :].astype(jnp.float32), scale)
+        return decode(incoming[pl.ds(MESSAGES[key][0] + at, size), :].astype(jnp.float32), scale)
 
     def got_within(key, at, size, scale):
         low, high = at // 16 * 16, -(-(at + size) // 16) * 16
@@ -233,16 +231,22 @@
     def lanes_of(p):
         return pl.ds(PARTS[p][3] * LANES, LANES)
 
+    bases = {}
+    for axis, stride in enumerate((16 * OWNED, 4 * OWNED, OWNED)):
+        for zero in range(2):
+            for one in range(2):
+                at = place[axis]
+                if zero:
+                    at = turn(at, 0, 1)
+                if one:
+                    at = turn(at, 1, 1)
+                bases[axis, zero, one] = at * stride
+
     def place_of(p, done, group, k):
         order = list(itertools.chain(*ORDERS[PARTS[p][0]][done:]))
-        at = list(place)
-        for i, (axis, kind) in enumerate(order):
-            weight = 1 << (len(order) - 1 - i)
-            if weight >= 4:
-                at[axis] = turn(at[axis], kind, lax.rem(lax.div(group, weight // 4), 2))
-            elif (k // weight) % 2:
-                at[axis] = turn(at[axis], kind, 1)
-        start = index_of(at) * OWNED + PARTS[p][1]
+        owner = 4 * group + k
+        bits = {t: (owner >> (len(order) - 1 - i)) & 1 for i, t in enumerate(order)}
+        start = PARTS[p][1] + sum(bases[a, bits.get((a, 0), 0), bits.get((a, 1), 0)] for a in range(3))
         return pl.ds(pl.multiple_of(start, 8), PARTS[p][2])
 
     def own(p, done, group, ks):
@@ -280,12 +284,8 @@
             bounds[p] = bound
             sent, inverse = to_send(bound)
             put_scale((p, 0, 1), sent)
-
-            def first(g, carry, p=p, rows=rows, inverse=inverse):
+            for g in range(8):
                 put((p, 0, 1), g * 4 * rows, own(p, 0, g + 8, ALL4), inverse)
-                return carry
-
-            lax.fori_loop(0, 8, first, 0)
             message((p, 0, 1)).start()
 
     nt = (((1,), (1,)), ((), ()))
@@ -375,20 +375,13 @@
                 block = flat(tiles(own(p, 1, g, ALL4)) * mine[None])
                 return block + got(came, g * 4 * rows, 4 * rows, scale)
 
-            def send(g, carry, p=p, rows=rows, inverse=inverse, summed=summed):
+            for g in range(4):
                 put((p, 1, 1), g * 4 * rows, summed(g + 4), inverse)
-                return carry
-
-            lax.fori_loop(0, 4, send, 0)
             message((p, 1, 1)).start()
             kept.append((p, summed))
         for p, summed in kept:
-
-            def hold(g, carry, p=p, summed=summed):
+            for g in range(4):
                 keep(p, 1, g, ALL4, summed(g))
-                return carry
-
-            lax.fori_loop(0, 4, hold, 0)
 
     def third(parts):
         kept = []

time: 56 us -> 53.9 us (0.963)
  Pallas kernels: 51.9 us -> 49.8 us
    pallas_call x1, Pallas kernels: 51.9 us -> 49.8 us  [on_device(): pl.pallas_call(functools.partial(kernel, threshold, factor), out_shape=(j...]
where the time goes in v2:
time: 53.9 us; the launch traced here: 53.7 us
  Pallas kernels  49.8 us (92%)
  between operations  2.39 us (4%)
  local copies, waits for them, and re-layouts  1.58 us (3%)
    pallas_call x1, Pallas kernels, on_device(): pl.pallas_call(functools.partial(kernel, threshold, factor), out_shape=(j...  49.8 us
    unnamed x1, local copies, waits for them, and re-layouts  1.58 us

profile of v2, /device:TPU:1, one launch (start us, length us, event | category | flops | bytes accessed | tf_op | source)
XLA Modules:
  0.0 53.7 jit_solution(17876375508874980737)
XLA Ops:
  0.6 49.8 %shard_map.59 = (f32[72,512]{1,0:T(8,128)}, f32[1]{0:T(128)}) custom-call(bf16[1,512,4608]{2,1,0:T(8,128)(2,1)} %mlp_in.1, bf16[1,512,9216]{2,1,0:T(8,128)(2,1)} %mlp_cot.1, bf16[1,512,512]{2,1,0:T(8,128)(2,1)} %heads_in.1, bf16[1,512,4608]{2,1,0:T(8,128)(2,1)} %out_cot.1), custom_call_target="tpu_custom_call" | custom-call | tf_op jit(solution)/shard_map/pallas_call | solution.py:496
  50.4 1.6 %copy.8 = f32[72,512]{1,0:T(8,128)} copy(f32[72,512]{1,0:T(8,128)} %get-tuple-element.4) | data formatting | bytes 294912

commit v3 on v2

--- a/solution.py
+++ b/solution.py
@@ -127,7 +127,8 @@
     c_buf,
     h_buf,
     o_buf,
-    prod,
+    prod_a,
+    prod_b,
     gram_x,
     gram_c,
     squares,
@@ -228,8 +229,13 @@
         sent = (bound * UP).astype(jnp.bfloat16)
         return sent, 1.0 / sent.astype(jnp.float32)
 
+    prods = (prod_a, prod_b)
+
     def lanes_of(p):
         return pl.ds(PARTS[p][3] * LANES, LANES)
+
+    def held(p):
+        return prods[PARTS[p][3] // 2], pl.ds(PARTS[p][3] % 2 * LANES, LANES)
 
     bases = {}
     for axis, stride in enumerate((16 * OWNED, 4 * OWNED, OWNED)):
@@ -250,14 +256,28 @@
         return pl.ds(pl.multiple_of(start, 8), PARTS[p][2])
 
     def own(p, done, group, ks):
-        return jnp.concatenate([prod[place_of(p, done, group, k), lanes_of(p)] for k in ks], axis=0)
+        ref, lanes = held(p)
+        return jnp.concatenate([ref[place_of(p, done, group, k), lanes] for k in ks], axis=0)
 
     def keep(p, done, group, ks, block):
         rows = PARTS[p][2]
+        ref, lanes = held(p)
         for i, k in enumerate(ks):
-            prod[place_of(p, done, group, k), lanes_of(p)] = block[i * rows : (i + 1) * rows]
+            ref[place_of(p, done, group, k), lanes] = block[i * rows : (i + 1) * rows]
 
     ALL4 = range(4)
+
+    def first(half):
+        for p in Z[half] + XY[half]:
+            rows = PARTS[p][2]
+            bound = jnp.maximum(largest[:, lanes_of(p)] * (1.0 / TOP), TINY)
+            bounds[p] = bound
+            sent, inverse = to_send(bound)
+            put_scale((p, 0, 1), sent)
+            for g in range(8):
+                put((p, 0, 1), g * 4 * rows, own(p, 0, g + 8, ALL4), inverse)
+            message((p, 0, 1)).start()
+
     h_copy.wait()
     for half in range(2):
         part = pl.ds(half * 256, 256)
@@ -270,7 +290,7 @@
                 (((0,), (0,)), ((), ())),
                 preferred_element_type=jnp.float32,
             )
-            prod[pl.ds(i * o_step, o_step), part] = block
+            prods[half][pl.ds(i * o_step, o_step), :] = block
             block = tiles(block)
             square = jnp.sum(block * block, axis=0)
             most = jnp.max(jnp.abs(block), axis=0)
@@ -278,15 +298,8 @@
             largest[:, part] = most if i == 0 else jnp.maximum(largest[:, part], most)
         if half == 0:
             pl.semaphore_wait(barrier, len(greeted))
-        for p in Z[half] + XY[half]:
-            rows = PARTS[p][2]
-            bound = jnp.maximum(largest[:, lanes_of(p)] * (1.0 / TOP), TINY)
-            bounds[p] = bound
-            sent, inverse = to_send(bound)
-            put_scale((p, 0, 1), sent)
-            for g in range(8):
-                put((p, 0, 1), g * 4 * rows, own(p, 0, g + 8, ALL4), inverse)
-            message((p, 0, 1)).start()
+        if half == 0:
+            first(0)
 
     nt = (((1,), (1,)), ((), ()))
 
@@ -351,6 +364,7 @@
         )
     for copy in norm_copies:
         copy.start()
+    first(1)
     for copy in norm_copies:
         copy.wait_recv()
     total = norms[:, 0] + norms[:, 1]
@@ -509,7 +523,8 @@
             pltpu.VMEM((SEQ, FF // 4), bf16),
             pltpu.VMEM((SEQ, COLS), bf16),
             pltpu.VMEM((SEQ, D), bf16),
-            pltpu.VMEM((D, COLS), f32),
+            pltpu.VMEM((D, 256), f32),
+            pltpu.VMEM((D, 256), f32),
             pltpu.VMEM((3, HALF, HALF), f32),
             pltpu.VMEM((3, HALF, HALF), f32),
             pltpu.VMEM((8, COLS), f32),

time: 53.9 us -> 53.4 us (level)
  no operation moved by 1% of the time
where the time goes in v3:
time: 53.4 us; the launch traced here: 53.3 us
  Pallas kernels  49.3 us (92%)
  between operations  2.39 us (4%)
  local copies, waits for them, and re-layouts  1.58 us (3%)
    pallas_call x1, Pallas kernels, on_device(): pl.pallas_call(functools.partial(kernel, threshold, factor), out_shape=(j...  49.3 us
    unnamed x1, local copies, waits for them, and re-layouts  1.58 us

profile of v3, /device:TPU:1, one launch (start us, length us, event | category | flops | bytes accessed | tf_op | source)
XLA Modules:
  0.0 53.3 jit_solution(9187500511914353904)
XLA Ops:
  0.6 49.3 %shard_map.59 = (f32[72,512]{1,0:T(8,128)}, f32[1]{0:T(128)}) custom-call(bf16[1,512,4608]{2,1,0:T(8,128)(2,1)} %mlp_in.1, bf16[1,512,9216]{2,1,0:T(8,128)(2,1)} %mlp_cot.1, bf16[1,512,512]{2,1,0:T(8,128)(2,1)} %heads_in.1, bf16[1,512,4608]{2,1,0:T(8,128)(2,1)} %out_cot.1), custom_call_target="tpu_custom_call" | custom-call | tf_op jit(solution)/shard_map/pallas_call | solution.py:510
  50.0 1.6 %copy.8 = f32[72,512]{1,0:T(8,128)} copy(f32[72,512]{1,0:T(8,128)} %get-tuple-element.4) | data formatting | bytes 294912

commit v4 on v3

--- a/solution.py
+++ b/solution.py
@@ -267,8 +267,8 @@
 
     ALL4 = range(4)
 
-    def first(half):
-        for p in Z[half] + XY[half]:
+    def first(parts):
+        for p in parts:
             rows = PARTS[p][2]
             bound = jnp.maximum(largest[:, lanes_of(p)] * (1.0 / TOP), TINY)
             bounds[p] = bound
@@ -298,8 +298,7 @@
             largest[:, part] = most if i == 0 else jnp.maximum(largest[:, part], most)
         if half == 0:
             pl.semaphore_wait(barrier, len(greeted))
-        if half == 0:
-            first(0)
+        first(Z[0] + XY[0] if half == 0 else Z[1])
 
     nt = (((1,), (1,)), ((), ()))
 
@@ -364,7 +363,7 @@
         )
     for copy in norm_copies:
         copy.start()
-    first(1)
+    first(XY[1])
     for copy in norm_copies:
         copy.wait_recv()
     total = norms[:, 0] + norms[:, 1]

time: 53.4 us -> 53.7 us (level)
  no operation moved by 1% of the time
where the time goes in v4:
time: 53.7 us; the launch traced here: 53.6 us
  Pallas kernels  49.6 us (92%)
  between operations  2.39 us (4%)
  local copies, waits for them, and re-layouts  1.58 us (3%)
    pallas_call x1, Pallas kernels, on_device(): pl.pallas_call(functools.partial(kernel, threshold, factor), out_shape=(j...  49.6 us
    unnamed x1, local copies, waits for them, and re-layouts  1.58 us

profile of v4, /device:TPU:1, one launch (start us, length us, event | category | flops | bytes accessed | tf_op | source)
XLA Modules:
  0.0 53.6 jit_solution(13084338878713757460)
XLA Ops:
  0.6 49.6 %shard_map.59 = (f32[72,512]{1,0:T(8,128)}, f32[1]{0:T(128)}) custom-call(bf16[1,512,4608]{2,1,0:T(8,128)(2,1)} %mlp_in.1, bf16[1,512,9216]{2,1,0:T(8,128)(2,1)} %mlp_cot.1, bf16[1,512,512]{2,1,0:T(8,128)(2,1)} %heads_in.1, bf16[1,512,4608]{2,1,0:T(8,128)(2,1)} %out_cot.1), custom_call_target="tpu_custom_call" | custom-call | tf_op jit(solution)/shard_map/pallas_call | solution.py:509
  50.3 1.6 %copy.8 = f32[72,512]{1,0:T(8,128)} copy(f32[72,512]{1,0:T(8,128)} %get-tuple-element.4) | data formatting | bytes 294912
